TPU v7x, 32 devices: a whole 2x2x4 slice. The times are simulated.
32 devices in a mesh: leaf: 4 (over y, x), row: 4 (over z), col: 2 (over core).
Axes of the slice: x: 2, y: 2, z: 4, core: 2. Of those that a mesh axis runs over, the one named last changes fastest.
Arguments:
- local_inv: float32 [4, 4, 32, 128, 128], P('leaf', 'row', 'col'), may hold values from -2 to 2, as said below
- local_off: float32 [4, 4, 32, 2, 128, 128], P('leaf', 'row', 'col'), may hold values from -0.09375 to 0.09375
- local_dep: int32 [4, 4, 32, 2], P('leaf', 'row', 'col'), may hold values from 0 to 7
- local_rhs: float32 [4, 4, 32, 64, 128], P('leaf', 'row', 'col'), may hold values from -6 to 6
- top_inv: float32 [8, 4, 2, 128, 128], P(None, 'row', 'col'), may hold values from -2 to 2, as said below
- top_off: float32 [7, 4, 2, 4, 128, 128], P(None, 'row', 'col'), may hold values from -0.125 to 0.125
- top_dep: int32 [7, 4, 2, 4], P(None, 'row', 'col'), may hold values from 0 to 5
- top_rhs: float32 [8, 4, 2, 64, 128], P(None, 'row', 'col'), may hold values from -6 to 6
Outputs:
- local_sol: float32 [4, 4, 32, 64, 128], P('leaf', 'row', 'col')
- top_sol: float32 [8, 4, 2, 64, 128], P(None, 'row', 'col')
Inputs may be any that keep to these rules, and one draw needn't show every extreme that they name: `local_inv`: lower-triangular inverse diagonal blocks of a Cholesky factor: entry [t, s] is zero for s > t. `top_inv`: lower-triangular inverse diagonal blocks of a Cholesky factor: entry [t, s] is zero for s > t. `local_dep`: levels of ancestors owned by the supernode's own grid cell. `top_dep`: a value v < 2 names the supernode one level lower in cell (r, v); a value v >= 2 the one in cell (v - 2, c).
All inputs are finite; a program needn't handle non-finite values.
Results may differ from a plain program's by a relative error of at most 0.0001.
Values sent between devices are 32-bit elements; how exact they have to be, the bound alone decides.
A program may use at most 64 MiB of HBM per device.

v0:
```python
import jax
import jax.numpy as jnp
from jax import lax
from jax.sharding import PartitionSpec as P

highest = lax.Precision.HIGHEST


def apply_inverse(inverse, block):
    return jnp.einsum("rs,ts->rt", block, inverse, precision=highest)


def apply_transpose(inverse, block):
    return jnp.einsum("rs,st->rt", block, inverse, precision=highest)


def select_rows(shard_rows, offsets):
    amount = shard_rows.shape[0]
    matches = (offsets[:, None] == jnp.arange(amount, dtype=jnp.int32)[None, :]).astype(jnp.float32)
    return jnp.einsum("jv,vrs->jrs", matches, shard_rows, precision=highest)


def spread_rows(pieces, offsets, amount):
    matches = (offsets[:, None] == jnp.arange(amount, dtype=jnp.int32)[None, :]).astype(jnp.float32)
    return jnp.einsum("jv,jrs->vrs", matches, pieces, precision=highest)


def gather_sources(block, sources, width_cols):
    picked = select_rows(lax.all_gather(block[None], "col", axis=0, tiled=True), sources)
    return picked + select_rows(
        lax.all_gather(block[None], "row", axis=0, tiled=True), sources - width_cols
    )


def push_back(pieces, sources, width_cols):
    from_cols = lax.psum_scatter(
        spread_rows(pieces, sources, 1 * lax.axis_size("col")),
        "col",
        scatter_dimension=0,
        tiled=True,
    )
    from_rows = lax.psum_scatter(
        spread_rows(pieces, sources - width_cols, 1 * lax.axis_size("row")),
        "row",
        scatter_dimension=0,
        tiled=True,
    )
    return from_cols[0] + from_rows[0]


def solve_top(top_inverse, top_blocks, top_links, top_right, updates):
    levels = top_inverse.shape[0]
    width_cols = lax.axis_size("col")
    forward = []
    for height in range(levels):
        target = top_right[height] - updates[height]
        if height > 0:
            picked = gather_sources(forward[-1], top_links[height - 1], width_cols)
            target = target - jnp.einsum(
                "jrs,jts->rt", picked, top_blocks[height - 1], precision=highest
            )
        forward.append(apply_inverse(top_inverse[height], target))
    backward = [None] * levels
    current = apply_transpose(top_inverse[levels - 1], forward[levels - 1])
    backward[levels - 1] = current
    for height in range(levels - 2, -1, -1):
        pieces = jnp.einsum("rt,jts->jrs", current, top_blocks[height], precision=highest)
        incoming = push_back(pieces, top_links[height], width_cols)
        current = apply_transpose(top_inverse[height], forward[height] - incoming)
        backward[height] = current
    return jnp.stack(backward)


def on_device(local_inv, local_off, local_dep, local_rhs, top_inv, top_off, top_dep, top_rhs):
    inverse = local_inv[0, 0]
    blocks = local_off[0, 0]
    ancestor_levels = local_dep[0, 0]
    right_local = local_rhs[0, 0]
    levels = top_inv.shape[0]
    top_inverse = top_inv[:, 0, 0]
    top_blocks = top_off[:, 0, 0]
    top_links = top_dep[:, 0, 0]
    top_right = top_rhs[:, 0, 0]
    local_first = jnp.einsum("krs,kts->krt", right_local, inverse, precision=highest)
    contributions = jnp.einsum("krs,kjts->kjrt", local_first, blocks, precision=highest)
    level_matches = (ancestor_levels[:, :, None] == jnp.arange(levels, dtype=jnp.int32)).astype(
        jnp.float32
    )
    updates = jnp.einsum("kjl,kjrt->lrt", level_matches, contributions, precision=highest)
    totals = lax.psum(updates, "leaf")
    top_solution = solve_top(top_inverse, top_blocks, top_links, top_right, totals)
    ancestors = jnp.einsum("kjl,lrt->kjrt", level_matches, top_solution, precision=highest)
    remainder = local_first - jnp.einsum("kjrt,kjts->krs", ancestors, blocks, precision=highest)
    local_solution = jnp.einsum("krs,kst->krt", remainder, inverse, precision=highest)
    return (local_solution[None, None], top_solution[:, None, None])


def solution(mesh):
    placed = (
        P("leaf", "row", "col", None, None),
        P("leaf", "row", "col", None, None, None),
        P("leaf", "row", "col", None),
        P("leaf", "row", "col", None, None),
        P(None, "row", "col", None, None),
        P(None, "row", "col", None, None, None),
        P(None, "row", "col", None),
        P(None, "row", "col", None, None),
    )
    return jax.shard_map(
        on_device,
        mesh=mesh,
        in_specs=placed,
        out_specs=(P("leaf", "row", "col", None, None), P(None, "row", "col", None, None)),
        check_vma=False,
    )
```

profile of v0, /device:TPU:0, one launch (start us, length us, event | category | flops | bytes accessed | tf_op | source)
XLA Modules:
  0.0 422.7 jit_solution(2540459524074262357)
XLA Ops:
  7.2 3.7 fusion.20
  10.9 2.3 fusion.2
  19.4 41.5 %all-reduce.2.cloned.1.call-done = f32[8,64,128]{2,0,1:T(8,128)} async-done(((f32[8,64,128]{2,0,1:T(8,128)}), f32[8,64,128]{2,0,1:T(8,128)}) %all-reduce.2.cloned.1.call-update) | async-done | bytes 262160 | tf_op jit(solution)/shard_map/psum | solution.py:90
  60.9 2.3 fusion.252
  63.5 13.4 %all-gather.1 = f32[256,128]{1,0:T(8,128)S(1)} all-gather(f32[64,128]{1,0:T(8,128)S(1)} %fusion.134), channel_id=3, replica_groups=mesh['leaf'=4,'row'=4,'col'=2] {'row'}, dimensions={0}, use_global_device_ids=true | all-gather | bytes 163840 | tf_op jit(solution)/shard_map/all_gather | solution.py:31
  76.9 1.8 all-gather
  81.7 13.6 %all-gather.3 = f32[256,128]{1,0:T(8,128)S(1)} all-gather(f32[64,128]{1,0:T(8,128)S(1)} %fusion.131), channel_id=5, replica_groups=mesh['leaf'=4,'row'=4,'col'=2] {'row'}, dimensions={0}, use_global_device_ids=true | all-gather | bytes 163840 | tf_op jit(solution)/shard_map/all_gather | solution.py:31
  95.3 1.8 all-gather.2
  98.5 13.4 %all-gather.5 = f32[256,128]{1,0:T(8,128)S(1)} all-gather(f32[64,128]{1,0:T(8,128)S(1)} %fusion.127), channel_id=7, replica_groups=mesh['leaf'=4,'row'=4,'col'=2] {'row'}, dimensions={0}, use_global_device_ids=true | all-gather | bytes 163840 | tf_op jit(solution)/shard_map/all_gather | solution.py:31
  112.0 1.8 all-gather.4
  115.2 13.4 %all-gather.7 = f32[256,128]{1,0:T(8,128)S(1)} all-gather(f32[64,128]{1,0:T(8,128)S(1)} %fusion.123), channel_id=9, replica_groups=mesh['leaf'=4,'row'=4,'col'=2] {'row'}, dimensions={0}, use_global_device_ids=true | all-gather | bytes 163840 | tf_op jit(solution)/shard_map/all_gather | solution.py:31
  128.6 1.8 all-gather.6
  131.8 13.4 %all-gather.9 = f32[256,128]{1,0:T(8,128)S(1)} all-gather(f32[64,128]{1,0:T(8,128)S(1)} %fusion.119), channel_id=11, replica_groups=mesh['leaf'=4,'row'=4,'col'=2] {'row'}, dimensions={0}, use_global_device_ids=true | all-gather | bytes 163840 | tf_op jit(solution)/shard_map/all_gather | solution.py:31
  148.3 13.4 %all-gather.11 = f32[256,128]{1,0:T(8,128)S(1)} all-gather(f32[64,128]{1,0:T(8,128)S(1)} %fusion.115), channel_id=13, replica_groups=mesh['leaf'=4,'row'=4,'col'=2] {'row'}, dimensions={0}, use_global_device_ids=true | all-gather | bytes 163840 | tf_op jit(solution)/shard_map/all_gather | solution.py:31
  161.7 1.8 all-gather.10
  164.9 13.4 %all-gather.13 = f32[256,128]{1,0:T(8,128)S(1)} all-gather(f32[64,128]{1,0:T(8,128)S(1)} %fusion.111), channel_id=15, replica_groups=mesh['leaf'=4,'row'=4,'col'=2] {'row'}, dimensions={0}, use_global_device_ids=true | all-gather | bytes 163840 | tf_op jit(solution)/shard_map/all_gather | solution.py:31
  178.3 2.0 all-gather.12
  184.9 6.4 %reduce-scatter.15.cloned.1.call-done = f32[1,64,128]{2,1,0:T(8,128)} async-done(((f32[2,64,128]{2,1,0:T(8,128)}), f32[1,64,128]{2,1,0:T(8,128)}) %reduce-scatter.15.cloned.1.call-update) | async-done | bytes 32784 | tf_op jit(solution)/shard_map/reduce_scatter | solution.py:36
  191.3 23.3 %reduce-scatter.17.cloned.1.call-done = f32[1,64,128]{2,1,0:T(8,128)} async-done(((f32[4,64,128]{2,1,0:T(8,128)}), f32[1,64,128]{2,1,0:T(8,128)}) %reduce-scatter.17.cloned.1.call-update) | async-done | bytes 32784 | tf_op jit(solution)/shard_map/reduce_scatter | solution.py:42
  220.7 4.1 reduce-scatter.19.cloned.1.call-done
  224.8 23.1 %reduce-scatter.21.cloned.1.call-done = f32[1,64,128]{2,1,0:T(8,128)} async-done(((f32[4,64,128]{2,1,0:T(8,128)}), f32[1,64,128]{2,1,0:T(8,128)}) %reduce-scatter.21.cloned.1.call-update) | async-done | bytes 32784 | tf_op jit(solution)/shard_map/reduce_scatter | solution.py:42
  253.5 3.9 reduce-scatter.23.cloned.1.call-done
  257.4 23.3 %reduce-scatter.25.cloned.1.call-done = f32[1,64,128]{2,1,0:T(8,128)} async-done(((f32[4,64,128]{2,1,0:T(8,128)}), f32[1,64,128]{2,1,0:T(8,128)}) %reduce-scatter.25.cloned.1.call-update) | async-done | bytes 32784 | tf_op jit(solution)/shard_map/reduce_scatter | solution.py:42
  285.6 4.0 reduce-scatter.27.cloned.1.call-done
  289.6 23.2 %reduce-scatter.29.cloned.1.call-done = f32[1,64,128]{2,1,0:T(8,128)} async-done(((f32[4,64,128]{2,1,0:T(8,128)}), f32[1,64,128]{2,1,0:T(8,128)}) %reduce-scatter.29.cloned.1.call-update) | async-done | bytes 32784 | tf_op jit(solution)/shard_map/reduce_scatter | solution.py:42
  317.8 4.0 reduce-scatter.31.cloned.1.call-done
  321.8 23.3 %reduce-scatter.33.cloned.1.call-done = f32[1,64,128]{2,1,0:T(8,128)} async-done(((f32[4,64,128]{2,1,0:T(8,128)}), f32[1,64,128]{2,1,0:T(8,128)}) %reduce-scatter.33.cloned.1.call-update) | async-done | bytes 32784 | tf_op jit(solution)/shard_map/reduce_scatter | solution.py:42
  350.0 4.0 reduce-scatter.35.cloned.1.call-done
  354.1 23.2 %reduce-scatter.37.cloned.1.call-done = f32[1,64,128]{2,1,0:T(8,128)} async-done(((f32[4,64,128]{2,1,0:T(8,128)}), f32[1,64,128]{2,1,0:T(8,128)}) %reduce-scatter.37.cloned.1.call-update) | async-done | bytes 32784 | tf_op jit(solution)/shard_map/reduce_scatter | solution.py:42
  382.1 4.7 %reduce-scatter.39.cloned.1.call-done = f32[1,64,128]{2,1,0:T(8,128)} async-done(((f32[2,64,128]{2,1,0:T(8,128)}), f32[1,64,128]{2,1,0:T(8,128)}) %reduce-scatter.39.cloned.1.call-update) | async-done | bytes 32784 | tf_op jit(solution)/shard_map/reduce_scatter | solution.py:36
  386.8 23.2 %reduce-scatter.41.cloned.1.call-done = f32[1,64,128]{2,1,0:T(8,128)} async-done(((f32[4,64,128]{2,1,0:T(8,128)}), f32[1,64,128]{2,1,0:T(8,128)}) %reduce-scatter.41.cloned.1.call-update) | async-done | bytes 32784 | tf_op jit(solution)/shard_map/reduce_scatter | solution.py:42
  414.2 1.9 convolution_bitcast_fusion
  (173 shorter events, 57.3 us)
Async XLA Ops:
  7.2 53.7 %all-reduce.2.cloned.1.call-start = ((), (), s32[]{:S(2)}) async-start(), calls=%async_computation.14 | async-start | bytes 524288 | tf_op jit(solution)/shard_map/psum | solution.py:90
  13.3 50.0 %copy-start.3 = (f32[8,1,1,128,128]{4,3,2,1,0:T(8,128)S(1)}, f32[8,1,1,128,128]{4,3,2,1,0:T(8,128)}, u32[]{:S(2)}) copy-start(f32[8,1,1,128,128]{4,3,2,1,0:T(8,128)} %param.12) | copy-start | bytes 1572868
  13.3 50.0 %copy-start.8 = (f32[8,1,1,64,128]{4,3,2,1,0:T(8,128)S(1)}, f32[8,1,1,64,128]{4,3,2,1,0:T(8,128)}, u32[]{:S(2)}) copy-start(f32[8,1,1,64,128]{4,3,2,1,0:T(8,128)} %param.15) | copy-start | bytes 786436
  15.1 176.2 %reduce-scatter.15.cloned.1.call-start = ((), (), s32[]{:S(2)}) async-start(), calls=%async_computation.15 | async-start | bytes 98304 | tf_op jit(solution)/shard_map/reduce_scatter | solution.py:36
  15.4 47.8 %copy-start.11 = (s32[4]{0:T(128)}, s32[4]{0:T(128)S(1)}, u32[]{:S(2)}) copy-start(s32[4]{0:T(128)S(1)} %get-tuple-element.5) | copy-start | bytes 52
  15.5 47.8 %copy-start.13 = (s32[4]{0:T(128)}, s32[4]{0:T(128)S(1)}, u32[]{:S(2)}) copy-start(s32[4]{0:T(128)S(1)} %get-tuple-element.10) | copy-start | bytes 52
  15.5 47.8 %copy-start.15 = (s32[4]{0:T(128)}, s32[4]{0:T(128)S(1)}, u32[]{:S(2)}) copy-start(s32[4]{0:T(128)S(1)} %get-tuple-element.4) | copy-start | bytes 52
  63.2 50.9 %copy-start.21 = (s32[4]{0:T(128)S(1)}, s32[4]{0:T(128)}, u32[]{:S(2)}) copy-start(s32[4]{0:T(128)} %broadcast_add_fusion.4) | copy-start | bytes 52
  81.5 49.3 %copy-start.22 = (s32[4]{0:T(128)S(1)}, s32[4]{0:T(128)}, u32[]{:S(2)}) copy-start(s32[4]{0:T(128)} %broadcast_add_fusion.3) | copy-start | bytes 52
  81.7 49.4 %copy-start.9 = (f32[8,1,1,64,128]{4,3,2,1,0:T(8,128)S(1)}, f32[8,1,1,64,128]{4,3,2,1,0:T(8,128)}, u32[]{:S(2)}) copy-start(f32[8,1,1,64,128]{4,3,2,1,0:T(8,128)} %param.15) | copy-start | bytes 786436
  98.3 48.8 %copy-start.12 = (s32[4]{0:T(128)S(1)}, s32[4]{0:T(128)}, u32[]{:S(2)}) copy-start(s32[4]{0:T(128)} %copy-done.11) | copy-start | bytes 52
  98.3 49.1 %copy-start.23 = (s32[4]{0:T(128)S(1)}, s32[4]{0:T(128)}, u32[]{:S(2)}) copy-start(s32[4]{0:T(128)} %broadcast_add_fusion.2) | copy-start | bytes 52
  114.9 48.7 %copy-start.14 = (s32[4]{0:T(128)S(1)}, s32[4]{0:T(128)}, u32[]{:S(2)}) copy-start(s32[4]{0:T(128)} %copy-done.13) | copy-start | bytes 52
  114.9 49.0 %copy-start.24 = (s32[4]{0:T(128)S(1)}, s32[4]{0:T(128)}, u32[]{:S(2)}) copy-start(s32[4]{0:T(128)} %broadcast_add_fusion.1) | copy-start | bytes 52
  131.5 48.8 %copy-start.16 = (s32[4]{0:T(128)S(1)}, s32[4]{0:T(128)}, u32[]{:S(2)}) copy-start(s32[4]{0:T(128)} %copy-done.15) | copy-start | bytes 52
  131.5 49.1 %copy-start.25 = (s32[4]{0:T(128)S(1)}, s32[4]{0:T(128)}, u32[]{:S(2)}) copy-start(s32[4]{0:T(128)} %broadcast_add_fusion) | copy-start | bytes 52
  183.1 31.5 %reduce-scatter.17.cloned.1.call-start = ((), (), s32[]{:S(2)}) async-start(), calls=%async_computation.16 | async-start | bytes 163840 | tf_op jit(solution)/shard_map/reduce_scatter | solution.py:42
  184.8 39.9 %reduce-scatter.19.cloned.1.call-start = ((), (), s32[]{:S(2)}) async-start(), calls=%async_computation.17 | async-start | bytes 98304 | tf_op jit(solution)/shard_map/reduce_scatter | solution.py:36
  218.9 28.9 %reduce-scatter.21.cloned.1.call-start = ((), (), s32[]{:S(2)}) async-start(), calls=%async_computation.18 | async-start | bytes 163840 | tf_op jit(solution)/shard_map/reduce_scatter | solution.py:42
  220.7 36.8 %reduce-scatter.23.cloned.1.call-start = ((), (), s32[]{:S(2)}) async-start(), calls=%async_computation.19 | async-start | bytes 98304 | tf_op jit(solution)/shard_map/reduce_scatter | solution.py:36
  251.7 29.1 %reduce-scatter.25.cloned.1.call-start = ((), (), s32[]{:S(2)}) async-start(), calls=%async_computation.20 | async-start | bytes 163840 | tf_op jit(solution)/shard_map/reduce_scatter | solution.py:42
  253.4 36.2 %reduce-scatter.27.cloned.1.call-start = ((), (), s32[]{:S(2)}) async-start(), calls=%async_computation.21 | async-start | bytes 98304 | tf_op jit(solution)/shard_map/reduce_scatter | solution.py:36
  283.9 28.9 %reduce-scatter.29.cloned.1.call-start = ((), (), s32[]{:S(2)}) async-start(), calls=%async_computation.22 | async-start | bytes 163840 | tf_op jit(solution)/shard_map/reduce_scatter | solution.py:42
  285.6 36.3 %reduce-scatter.31.cloned.1.call-start = ((), (), s32[]{:S(2)}) async-start(), calls=%async_computation.23 | async-start | bytes 98304 | tf_op jit(solution)/shard_map/reduce_scatter | solution.py:36
  315.0 66.1 %copy-start.19 = (s32[4]{0:T(128)S(1)}, s32[4]{0:T(128)}, u32[]{:S(2)}) copy-start(s32[4]{0:T(128)} %broadcast_add_fusion.6) | copy-start | bytes 52
  316.0 29.1 %reduce-scatter.33.cloned.1.call-start = ((), (), s32[]{:S(2)}) async-start(), calls=%async_computation.24 | async-start | bytes 163840 | tf_op jit(solution)/shard_map/reduce_scatter | solution.py:42
  317.8 36.3 %reduce-scatter.35.cloned.1.call-start = ((), (), s32[]{:S(2)}) async-start(), calls=%async_computation.25 | async-start | bytes 98304 | tf_op jit(solution)/shard_map/reduce_scatter | solution.py:36
  346.1 65.7 %copy-start.6 = (f32[64,128]{1,0:T(8,128)S(1)}, f32[64,128]{1,0:T(8,128)}, u32[]{:S(2)}) copy-start(f32[64,128]{1,0:T(8,128)} %copy-done.5) | copy-start | bytes 98308
  346.1 65.7 %copy-start.18 = (s32[1,1,16,2]{2,3,1,0:T(2,128)S(1)}, s32[1,1,16,2]{2,3,1,0:T(2,128)}, u32[]{:S(2)}) copy-start(s32[1,1,16,2]{2,3,1,0:T(2,128)} %param.10) | copy-start | bytes 388
  348.3 28.9 %reduce-scatter.37.cloned.1.call-start = ((), (), s32[]{:S(2)}) async-start(), calls=%async_computation.26 | async-start | bytes 163840 | tf_op jit(solution)/shard_map/reduce_scatter | solution.py:42
  350.0 36.8 %reduce-scatter.39.cloned.1.call-start = ((), (), s32[]{:S(2)}) async-start(), calls=%async_computation.27 | async-start | bytes 98304 | tf_op jit(solution)/shard_map/reduce_scatter | solution.py:36
  381.0 28.9 %reduce-scatter.41.cloned.1.call-start = ((), (), s32[]{:S(2)}) async-start(), calls=%async_computation.28 | async-start | bytes 163840 | tf_op jit(solution)/shard_map/reduce_scatter | solution.py:42
  (9 other events, 89.4 us)
Sparse Core Ops, SparseCore 0:
  15.2 45.6 all-reduce.1
  183.2 8.0 reduce-scatter.14
  194.2 20.3 reduce-scatter.16
  219.1 5.6 reduce-scatter.18
  227.4 20.3 reduce-scatter.20
  251.8 5.5 reduce-scatter.22
  260.3 20.3 reduce-scatter.24
  284.0 5.5 reduce-scatter.26
  292.4 20.3 reduce-scatter.28
  316.1 5.6 reduce-scatter.30
  324.7 20.3 reduce-scatter.32
  348.4 5.5 reduce-scatter.34
  356.9 20.3 reduce-scatter.36
  381.1 5.5 reduce-scatter.38
  389.5 20.3 reduce-scatter.40
where the time goes:
time: 424 us; the launch traced here: 423 us
  waiting for transfers between devices  235 us (55%)
  blocking collectives  107 us (25%)
  matrix products  47.1 us (11%)
  between operations  14.8 us (3%)
  local copies, waits for them, and re-layouts  13.8 us (3%)
    reduce_scatter x7, waiting for transfers between devices, push_back(): lax.psum_scatter(spread_rows(pieces, sources - width_cols, 1 * lax.axis_s...  162 us
    all_gather x7, blocking collectives, gather_sources(): lax.all_gather(block[None], 'row', axis=0, tiled=True)  94 us
    psum x1, waiting for transfers between devices, on_device(): totals = lax.psum(updates, 'leaf')  41.5 us
    reduce_scatter x7, waiting for transfers between devices, push_back(): lax.psum_scatter(spread_rows(pieces, sources, 1 * lax.axis_size('col')),...  31.2 us
    all_gather x7, blocking collectives, gather_sources(): lax.all_gather(block[None], 'col', axis=0, tiled=True)  13.1 us
    dot_general x14, matrix products, spread_rows(): return jnp.einsum('jv,jrs->vrs', matches, pieces, precision=highest)  9.66 us
    dot_general x14, local copies, waits for them, and re-layouts, spread_rows(): return jnp.einsum('jv,jrs->vrs', matches, pieces, precision=highest)  9.1 us
  transfers between devices with their start and end apart: 15, of which 15 were waited for; matrix products, arithmetic and copies ran while one was open for 4% of the time, Pallas kernels for 0%

commit v1 on v0

v1 whole, which is shorter than its diff:
```python
import functools

import jax
import jax.numpy as jnp
from jax import lax
from jax.experimental import pallas as pl
from jax.experimental.pallas import tpu as pltpu
from jax.sharding import PartitionSpec as P

MESH = pl.DeviceIdType.MESH
f32 = jnp.float32
bf16 = jnp.bfloat16
NN = (((1,), (0,)), ((), ()))
NT = (((1,), (1,)), ((), ()))


def split(x):
    high = x.astype(bf16)
    return high, (x - high.astype(f32)).astype(bf16)


def dot3(a, b, dims):
    rows = a.shape[0]
    ah, al = split(a)
    bh, bl = b
    both = lax.dot_general(jnp.concatenate([ah, al], axis=0), bh, dims, preferred_element_type=f32)
    cross = lax.dot_general(ah, bl, dims, preferred_element_type=f32)
    return both[:rows] + both[rows:] + cross


def kernel(
    sizes, chunk,
    ldep, tdep, inv_h, off_h, rhs_h, tinv_h, toff_h, trhs_h,
    lsol_h, tsol_h,
    inv, off, rhs, tinv, toff, trhs, first, upd, rs, ybuf, yown, bout, bin_, tsol, lsol,
    wh, wl, vh, vl,
    in_sem, out_sem, rs_send, rs_recv, f_send, f_recv, b_send, b_recv, ag_send, ag_recv,
):
    n_leaf, n_row, n_col = sizes
    loc, s = inv.shape[0], inv.shape[1]
    fan = off.shape[1] // s
    levels, r = upd.shape[0], upd.shape[1]
    dep = tdep.shape[1]
    part = r // n_leaf
    slots = n_col + n_row
    q, me_r, me_c = lax.axis_index("leaf"), lax.axis_index("row"), lax.axis_index("col")
    leaf_peers = [lax.rem(q + d, n_leaf) for d in range(1, n_leaf)]
    row_peers = [lax.rem(me_r + d, n_row) for d in range(1, n_row)]
    col_peers = [lax.rem(me_c + d, n_col) for d in range(1, n_col)]
    at_leaf = [(p, me_r, me_c) for p in leaf_peers]
    at_row = [(q, p, me_c) for p in row_peers]
    at_col = [(q, me_r, p) for p in col_peers]

    def rows_of(p):
        return pl.ds(pl.multiple_of(p * part, part), part)

    mine = rows_of(q)

    n_chunks = loc // chunk
    loads = []
    for c in range(n_chunks):
        ks = pl.ds(c * chunk, chunk)
        for place, (src, dst) in enumerate(((rhs_h, rhs), (inv_h, inv), (off_h, off))):
            loads.append(pltpu.make_async_copy(src.at[ks], dst.at[ks], in_sem.at[3 * c + place]))
    late = 3 * n_chunks
    top_loads = [
        pltpu.make_async_copy(tinv_h, tinv, in_sem.at[late]),
        pltpu.make_async_copy(trhs_h.at[:, mine], trhs, in_sem.at[late + 1]),
        pltpu.make_async_copy(toff_h, toff, in_sem.at[late + 2]),
    ]
    for load in loads + top_loads:
        load.start()

    barrier = pltpu.get_barrier_semaphore()
    for peer in at_leaf + at_row + at_col:
        pl.semaphore_signal(barrier, inc=1, device_id=peer, device_id_type=MESH)

    for c in range(n_chunks):
        for load in loads[3 * c:3 * c + 3]:
            load.wait()
        contributions = []
        for k in range(c * chunk, (c + 1) * chunk):
            y = dot3(rhs[k], split(inv[k]), NT)
            first[k] = y
            both = dot3(y, split(off[k]), NT)
            for j in range(fan):
                contributions.append((ldep[k, j], both[:, j * s:(j + 1) * s]))
        for l in range(levels):
            total = None
            for level, block in contributions:
                term = jnp.where(level == l, 1.0, 0.0) * block
                total = term if total is None else total + term
            upd[l] = total if c == 0 else upd[l] + total

    pl.semaphore_wait(barrier, n_leaf + n_row + n_col - 3)

    def rs_copy(half, p, slot, device):
        ls = pl.ds(0, 1) if half == 0 else pl.ds(1, levels - 1)
        return pltpu.make_async_remote_copy(
            src_ref=upd.at[ls, rows_of(p)], dst_ref=rs.at[slot, ls],
            send_sem=rs_send.at[half, p], recv_sem=rs_recv.at[half, slot],
            device_id=device, device_id_type=MESH,
        )

    for half in range(2):
        for p, device in zip(leaf_peers, at_leaf):
            rs_copy(half, p, q, device).start()
    rs[q] = upd[:, mine]

    def local_fold(k):
        both = dot3(jnp.concatenate([off[k], first[k]], axis=0), split(inv[k]), NN)
        high, low = split(both[:fan * s])
        vh[k] = high
        vl[k] = low
        first[k] = both[fan * s:]

    for load in top_loads:
        load.wait()
    per_gap = loc // (levels - 1)
    early = loc - per_gap * (levels - 1)
    for k in range(early):
        local_fold(k)

    def rs_wait(half):
        for p, device in zip(leaf_peers, at_leaf):
            rs_copy(half, p, p, device).wait_recv()

    def own_part(l):
        z = trhs[l]
        for p in range(n_leaf):
            z = z - rs[p, l]
        return dot3(z, split(tinv[l]), NT)

    def f_copy(l, slot, device):
        return pltpu.make_async_remote_copy(
            src_ref=ybuf.at[l, slot], dst_ref=ybuf.at[l, slot],
            send_sem=f_send.at[l, device[0]], recv_sem=f_recv.at[l, slot],
            device_id=device[1], device_id_type=MESH,
        )

    col_out = [(p, d) for p, d in zip(col_peers, at_col)]
    row_out = [(n_col + p, d) for p, d in zip(row_peers, at_row)]

    def f_start(l, y):
        ybuf[l, me_c] = y
        ybuf[l, n_col + me_r] = y
        for target in row_out:
            f_copy(l, n_col + me_r, target).start()
        for target in col_out:
            f_copy(l, me_c, target).start()

    rs_wait(0)
    y = own_part(0)
    yown[0] = y
    f_start(0, y)
    rs_wait(1)

    def fold(l):
        inverse = tinv[l]
        for j in range(dep):
            high, low = split(dot3(inverse, split(toff[l - 1, j * s:(j + 1) * s]), NN))
            wh[l - 1, :, j * s:(j + 1) * s] = high
            wl[l - 1, :, j * s:(j + 1) * s] = low

    def up(l, y):
        fold(l)
        own = own_part(l)
        picks = [
            [jnp.where(tdep[l - 1, j] == slot, 1.0, 0.0) for slot in range(slots)]
            for j in range(dep)
        ]
        for slot, device in col_out + row_out:
            f_copy(l - 1, slot, (slot, device)).wait_recv()
        blocks = [ybuf[l - 1, slot] for slot in range(slots)]
        picked = []
        for j in range(dep):
            total = None
            for slot in range(slots):
                term = picks[j][slot] * blocks[slot]
                total = term if total is None else total + term
            picked.append(total)
        return own - dot3(jnp.concatenate(picked, axis=1), (wh[l - 1], wl[l - 1]), NT)

    def forward(l, y):
        y = up(l, y)
        yown[l] = y
        f_start(l, y)
        return y

    y = lax.fori_loop(1, levels - 1, forward, y)
    d = up(levels - 1, y)

    def ag_copy(l, p, owner, device):
        return pltpu.make_async_remote_copy(
            src_ref=tsol.at[l, rows_of(owner)], dst_ref=tsol.at[l, rows_of(owner)],
            send_sem=ag_send.at[l, p], recv_sem=ag_recv.at[l, owner],
            device_id=device, device_id_type=MESH,
        )

    def publish(l, d):
        tsol[l, mine] = dot3(d, split(tinv[l]), NN)
        for p, device in zip(leaf_peers, at_leaf):
            ag_copy(l, p, q, device).start()

    def b_copy(l, slot, landing, device):
        return pltpu.make_async_remote_copy(
            src_ref=bout.at[l, slot], dst_ref=bin_.at[l, landing],
            send_sem=b_send.at[l, slot], recv_sem=b_recv.at[l, landing],
            device_id=device, device_id_type=MESH,
        )

    def backward(step, d):
        l = levels - 1 - step
        pieces = dot3(d, (wh[l - 1], wl[l - 1]), NN)
        sources = [tdep[l - 1, j] for j in range(dep)]
        for slot in range(slots):
            total = None
            for j in range(dep):
                term = jnp.where(sources[j] == slot, 1.0, 0.0) * pieces[:, j * s:(j + 1) * s]
                total = term if total is None else total + term
            bout[l - 1, slot] = total
        for slot, device in row_out:
            b_copy(l - 1, slot, n_col + me_r, device).start()
        for slot, device in col_out:
            b_copy(l - 1, slot, me_c, device).start()
        bin_[l - 1, me_c] = bout[l - 1, me_c]
        bin_[l - 1, n_col + me_r] = bout[l - 1, n_col + me_r]
        publish(l, d)
        for extra in range(per_gap):
            local_fold(early + step * per_gap + extra)
        for slot, device in col_out + row_out:
            b_copy(l - 1, slot, slot, device).wait_recv()
        total = bin_[l - 1, 0]
        for slot in range(1, slots):
            total = total + bin_[l - 1, slot]
        return yown[l - 1] - total

    d = lax.fori_loop(0, levels - 1, backward, d)
    publish(0, d)

    def ag_wait(l, carry):
        for p, device in zip(leaf_peers, at_leaf):
            ag_copy(l, p, p, device).wait_recv()
        return carry

    lax.fori_loop(0, levels, ag_wait, 0)
    top_out = pltpu.make_async_copy(tsol, tsol_h, out_sem.at[n_chunks])
    top_out.start()

    outs = []
    for c in range(n_chunks):
        ks = pl.ds(c * chunk, chunk)
        for k in range(c * chunk, (c + 1) * chunk):
            above = jnp.concatenate([tsol[ldep[k, j]] for j in range(fan)], axis=1)
            lsol[k] = first[k] - dot3(above, (vh[k], vl[k]), NN)
        outs.append(pltpu.make_async_copy(lsol.at[ks], lsol_h.at[ks], out_sem.at[c]))
        outs[-1].start()

    for half in range(2):
        for p, device in zip(leaf_peers, at_leaf):
            rs_copy(half, p, q, device).wait_send()

    def drain(l, carry):
        for target in row_out:
            f_copy(l, n_col + me_r, target).wait_send()
        for target in col_out:
            f_copy(l, me_c, target).wait_send()
        for slot, device in row_out + col_out:
            b_copy(l, slot, slot, device).wait_send()
        return carry

    lax.fori_loop(0, levels - 1, drain, 0)

    def drain_ag(l, carry):
        for p, device in zip(leaf_peers, at_leaf):
            ag_copy(l, p, q, device).wait_send()
        return carry

    lax.fori_loop(0, levels, drain_ag, 0)
    for out in outs + [top_out]:
        out.wait()


def on_device(sizes, local_inv, local_off, local_dep, local_rhs, top_inv, top_off, top_dep, top_rhs):
    n_leaf, n_row, n_col = sizes
    loc, s = local_inv.shape[2], local_inv.shape[3]
    fan = local_off.shape[3]
    r = local_rhs.shape[3]
    levels, dep = top_inv.shape[0], top_off.shape[3]
    part, slots = r // n_leaf, n_row + n_col
    chunk = 4 if loc % 4 == 0 else 1
    n_chunks = loc // chunk
    hbm = pl.BlockSpec(memory_space=pl.ANY)
    smem = pl.BlockSpec(memory_space=pltpu.SMEM)
    dma = pltpu.SemaphoreType.DMA
    local_sol, top_sol = pl.pallas_call(
        functools.partial(kernel, sizes, chunk),
        out_shape=(
            jax.ShapeDtypeStruct((loc, r, s), f32),
            jax.ShapeDtypeStruct((levels, r, s), f32),
        ),
        in_specs=[smem, smem] + [hbm] * 6,
        out_specs=(hbm, hbm),
        scratch_shapes=[
            pltpu.VMEM((loc, s, s), f32),
            pltpu.VMEM((loc, fan * s, s), f32),
            pltpu.VMEM((loc, r, s), f32),
            pltpu.VMEM((levels, s, s), f32),
            pltpu.VMEM((levels - 1, dep * s, s), f32),
            pltpu.VMEM((levels, part, s), f32),
            pltpu.VMEM((loc, r, s), f32),
            pltpu.VMEM((levels, r, s), f32),
            pltpu.VMEM((n_leaf, levels, part, s), f32),
            pltpu.VMEM((levels - 1, slots, part, s), f32),
            pltpu.VMEM((levels, part, s), f32),
            pltpu.VMEM((levels - 1, slots, part, s), f32),
            pltpu.VMEM((levels - 1, slots, part, s), f32),
            pltpu.VMEM((levels, r, s), f32),
            pltpu.VMEM((loc, r, s), f32),
            pltpu.VMEM((levels - 1, s, dep * s), bf16),
            pltpu.VMEM((levels - 1, s, dep * s), bf16),
            pltpu.VMEM((loc, fan * s, s), bf16),
            pltpu.VMEM((loc, fan * s, s), bf16),
            dma((3 * n_chunks + 3,)),
            dma((n_chunks + 1,)),
            dma((2, n_leaf)),
            dma((2, n_leaf)),
            dma((levels - 1, slots)),
            dma((levels - 1, slots)),
            dma((levels - 1, slots)),
            dma((levels - 1, slots)),
            dma((levels, n_leaf)),
            dma((levels, n_leaf)),
        ],
        compiler_params=pltpu.CompilerParams(
            collective_id=0, has_side_effects=True, vmem_limit_bytes=40 * 2**20
        ),
    )(
        local_dep.reshape(loc, fan),
        top_dep.reshape(levels - 1, dep),
        local_inv.reshape(loc, s, s),
        local_off.reshape(loc, fan * s, s),
        local_rhs.reshape(loc, r, s),
        top_inv.reshape(levels, s, s),
        top_off.reshape(levels - 1, dep * s, s),
        top_rhs.reshape(levels, r, s),
    )
    return local_sol[None, None], top_sol[:, None, None]


def solution(mesh):
    placed = (
        P("leaf", "row", "col", None, None),
        P("leaf", "row", "col", None, None, None),
        P("leaf", "row", "col", None),
        P("leaf", "row", "col", None, None),
        P(None, "row", "col", None, None),
        P(None, "row", "col", None, None, None),
        P(None, "row", "col", None),
        P(None, "row", "col", None, None),
    )
    sizes = (mesh.shape["leaf"], mesh.shape["row"], mesh.shape["col"])
    return jax.shard_map(
        functools.partial(on_device, sizes),
        mesh=mesh,
        in_specs=placed,
        out_specs=(P("leaf", "row", "col", None, None), P(None, "row", "col", None, None)),
        check_vma=False,
    )
```

time: 424 us -> 83.9 us (0.20)
  waiting for transfers between devices: 235 us -> 0 us
  blocking collectives: 107 us -> 0 us
  Pallas kernels: 0 us -> 72.5 us
  matrix products: 47.1 us -> 0 us
  between operations: 14.8 us -> 0.65 us
    reduce_scatter x14 -> x0, waiting for transfers between devices: 194 us -> none  [the longest x7 162 us: push_back(): lax.psum_scatter(spread_rows(pieces, sources - width_cols, 1 * lax.axis_s...]
    all_gather x14 -> x0, blocking collectives: 107 us -> none  [the longest x7 94 us: gather_sources(): lax.all_gather(block[None], 'row', axis=0, tiled=True)]
    pallas_call x0 -> x1, Pallas kernels: none -> 72.5 us  [on_device(): pl.pallas_call(functools.partial(kernel, sizes, chunk), out_shape=(jax.Sh...]
    dot_general x64 -> x0, matrix products: 47.1 us -> none  [the longest x14 9.66 us: spread_rows(): return jnp.einsum('jv,jrs->vrs', matches, pieces, precision=highest)]
    psum x1 -> x0, waiting for transfers between devices: 41.5 us -> none  [on_device(): totals = lax.psum(updates, 'leaf')]
    dot_general x14 -> x0, local copies, waits for them, and re-layouts: 9.1 us -> none  [spread_rows(): return jnp.einsum('jv,jrs->vrs', matches, pieces, precision=highest)]
    unnamed x58 -> x14, local copies, waits for them, and re-layouts: 2.1 us -> 8.84 us
  transfers between devices with their start and end apart: 15 -> 0, of which waited for: 15 -> 0; matrix products, arithmetic and copies ran while one was open for 4% -> 0% of each run, Pallas kernels for 0% -> 0%
where the time goes in v1:
time: 83.9 us; the launch traced here: 83.5 us
  Pallas kernels  72.5 us (86%)
  local copies, waits for them, and re-layouts  10.4 us (12%)
    pallas_call x1, Pallas kernels, on_device(): pl.pallas_call(functools.partial(kernel, sizes, chunk), out_shape=(jax.Sh...  72.5 us
    unnamed x14, local copies, waits for them, and re-layouts  8.84 us

profile of v1, /device:TPU:0, one launch (start us, length us, event | category | flops | bytes accessed | tf_op | source)
XLA Modules:
  0.0 83.5 jit_solution(2087636786497684207)
XLA Ops:
  0.6 0.8 copy.11.tdep
  1.4 0.8 copy.10.ldep
  2.2 0.0 copy-start
  2.2 1.6 %copy-done = f32[1,1,16,2,128,128]{5,4,3,2,1,0:T(8,128)S(1)} copy-done((f32[1,1,16,2,128,128]{5,4,3,2,1,0:T(8,128)S(1)}, f32[1,1,16,2,128,128]{5,4,3,2,1,0:T(8,128)}, u32[]{:S(2)}) %copy-start) | copy-done | bytes 2097176
  3.7 0.0 copy-start.1
  3.7 1.5 %copy-done.1 = f32[7,1,1,4,128,128]{5,4,3,2,1,0:T(8,128)S(1)} copy-done((f32[7,1,1,4,128,128]{5,4,3,2,1,0:T(8,128)S(1)}, f32[7,1,1,4,128,128]{5,4,3,2,1,0:T(8,128)}, u32[]{:S(2)}) %copy-start.1) | copy-done | bytes 1835032
  5.2 0.0 copy-start.2
  5.2 1.2 %copy-done.2 = f32[1,1,16,128,128]{4,3,2,1,0:T(8,128)S(1)} copy-done((f32[1,1,16,128,128]{4,3,2,1,0:T(8,128)S(1)}, f32[1,1,16,128,128]{4,3,2,1,0:T(8,128)}, u32[]{:S(2)}) %copy-start.2) | copy-done | bytes 1048600
  6.5 0.0 copy-start.3
  6.5 1.0 %copy-done.3 = f32[1,1,16,64,128]{4,3,2,1,0:T(8,128)S(1)} copy-done((f32[1,1,16,64,128]{4,3,2,1,0:T(8,128)S(1)}, f32[1,1,16,64,128]{4,3,2,1,0:T(8,128)}, u32[]{:S(2)}) %copy-start.3) | copy-done | bytes 524312
  7.5 0.0 copy-start.4
  7.5 1.0 %copy-done.4 = f32[8,1,1,128,128]{4,3,2,1,0:T(8,128)S(1)} copy-done((f32[8,1,1,128,128]{4,3,2,1,0:T(8,128)S(1)}, f32[8,1,1,128,128]{4,3,2,1,0:T(8,128)}, u32[]{:S(2)}) %copy-start.4) | copy-done | bytes 524312
  8.6 0.0 copy-start.5
  8.6 0.9 %copy-done.5 = f32[8,1,1,64,128]{4,3,2,1,0:T(8,128)S(1)} copy-done((f32[8,1,1,64,128]{4,3,2,1,0:T(8,128)S(1)}, f32[8,1,1,64,128]{4,3,2,1,0:T(8,128)}, u32[]{:S(2)}) %copy-start.5) | copy-done | bytes 262168
  9.5 72.5 %shard_map.95 = (f32[16,64,128]{2,1,0:T(8,128)S(1)}, f32[8,64,128]{2,1,0:T(8,128)S(1)}) custom-call(s32[16,2]{1,0:T(8,128)S(1)} %copy.10.ldep, s32[7,4]{1,0:T(8,128)S(1)} %copy.11.tdep, f32[16,128,128]{2,1,0:T(8,128)S(1)} %bitcast.14, f32[16,256,128]{2,1,0:T(8,128)S(1)} %bitcast.12, f32[16,64,128]{2,1,0:T(8,128)S(1)} %bitcast.16, ...), custom_call_target="tpu_custom_call" | custom-call | tf_op jit(solution)/shard_map/pallas_call | solution.py:296
  82.0 0.8 copy.15
  82.8 0.7 copy.16
Async XLA Ops:
  2.2 1.6 %copy-start = (f32[1,1,16,2,128,128]{5,4,3,2,1,0:T(8,128)S(1)}, f32[1,1,16,2,128,128]{5,4,3,2,1,0:T(8,128)}, u32[]{:S(2)}) copy-start(f32[1,1,16,2,128,128]{5,4,3,2,1,0:T(8,128)} %param.9) | copy-start | bytes 6291460
  3.7 1.5 %copy-start.1 = (f32[7,1,1,4,128,128]{5,4,3,2,1,0:T(8,128)S(1)}, f32[7,1,1,4,128,128]{5,4,3,2,1,0:T(8,128)}, u32[]{:S(2)}) copy-start(f32[7,1,1,4,128,128]{5,4,3,2,1,0:T(8,128)} %param.13) | copy-start | bytes 5505028
  5.2 1.2 %copy-start.2 = (f32[1,1,16,128,128]{4,3,2,1,0:T(8,128)S(1)}, f32[1,1,16,128,128]{4,3,2,1,0:T(8,128)}, u32[]{:S(2)}) copy-start(f32[1,1,16,128,128]{4,3,2,1,0:T(8,128)} %param.8) | copy-start | bytes 3145732
  6.5 1.0 %copy-start.3 = (f32[1,1,16,64,128]{4,3,2,1,0:T(8,128)S(1)}, f32[1,1,16,64,128]{4,3,2,1,0:T(8,128)}, u32[]{:S(2)}) copy-start(f32[1,1,16,64,128]{4,3,2,1,0:T(8,128)} %param.11) | copy-start | bytes 1572868
  7.5 1.0 %copy-start.4 = (f32[8,1,1,128,128]{4,3,2,1,0:T(8,128)S(1)}, f32[8,1,1,128,128]{4,3,2,1,0:T(8,128)}, u32[]{:S(2)}) copy-start(f32[8,1,1,128,128]{4,3,2,1,0:T(8,128)} %param.12) | copy-start | bytes 1572868
  8.6 0.9 %copy-start.5 = (f32[8,1,1,64,128]{4,3,2,1,0:T(8,128)S(1)}, f32[8,1,1,64,128]{4,3,2,1,0:T(8,128)}, u32[]{:S(2)}) copy-start(f32[8,1,1,64,128]{4,3,2,1,0:T(8,128)} %param.15) | copy-start | bytes 786436

commit v2 on v1

--- a/solution.py
+++ b/solution.py
@@ -26,6 +26,16 @@
     both = lax.dot_general(jnp.concatenate([ah, al], axis=0), bh, dims, preferred_element_type=f32)
     cross = lax.dot_general(ah, bl, dims, preferred_element_type=f32)
     return both[:rows] + both[rows:] + cross
+
+
+def farthest_first(me, n):
+    upper = (2 * me) // n
+    peers = []
+    for i in range(n - 1):
+        up = i + jnp.where(i >= me, 1, 0)
+        down = n - 1 - i - jnp.where(n - 1 - i <= me, 1, 0)
+        peers.append(upper * up + (1 - upper) * down)
+    return peers
 
 
 def kernel(
@@ -40,12 +50,12 @@
     loc, s = inv.shape[0], inv.shape[1]
     fan = off.shape[1] // s
     levels, r = upd.shape[0], upd.shape[1]
-    dep = tdep.shape[1]
+    dep = tdep.shape[0]
     part = r // n_leaf
     slots = n_col + n_row
     q, me_r, me_c = lax.axis_index("leaf"), lax.axis_index("row"), lax.axis_index("col")
     leaf_peers = [lax.rem(q + d, n_leaf) for d in range(1, n_leaf)]
-    row_peers = [lax.rem(me_r + d, n_row) for d in range(1, n_row)]
+    row_peers = farthest_first(me_r, n_row)
     col_peers = [lax.rem(me_c + d, n_col) for d in range(1, n_col)]
     at_leaf = [(p, me_r, me_c) for p in leaf_peers]
     at_row = [(q, p, me_c) for p in row_peers]
@@ -84,7 +94,7 @@
             first[k] = y
             both = dot3(y, split(off[k]), NT)
             for j in range(fan):
-                contributions.append((ldep[k, j], both[:, j * s:(j + 1) * s]))
+                contributions.append((ldep[j, k], both[:, j * s:(j + 1) * s]))
         for l in range(levels):
             total = None
             for level, block in contributions:
@@ -166,7 +176,7 @@
         fold(l)
         own = own_part(l)
         picks = [
-            [jnp.where(tdep[l - 1, j] == slot, 1.0, 0.0) for slot in range(slots)]
+            [jnp.where(tdep[j, l - 1] == slot, 1.0, 0.0) for slot in range(slots)]
             for j in range(dep)
         ]
         for slot, device in col_out + row_out:
@@ -212,7 +222,7 @@
     def backward(step, d):
         l = levels - 1 - step
         pieces = dot3(d, (wh[l - 1], wl[l - 1]), NN)
-        sources = [tdep[l - 1, j] for j in range(dep)]
+        sources = [tdep[j, l - 1] for j in range(dep)]
         for slot in range(slots):
             total = None
             for j in range(dep):
@@ -251,7 +261,7 @@
     for c in range(n_chunks):
         ks = pl.ds(c * chunk, chunk)
         for k in range(c * chunk, (c + 1) * chunk):
-            above = jnp.concatenate([tsol[ldep[k, j]] for j in range(fan)], axis=1)
+            above = jnp.concatenate([tsol[ldep[j, k]] for j in range(fan)], axis=1)
             lsol[k] = first[k] - dot3(above, (vh[k], vl[k]), NN)
         outs.append(pltpu.make_async_copy(lsol.at[ks], lsol_h.at[ks], out_sem.at[c]))
         outs[-1].start()
@@ -333,11 +343,11 @@
             dma((levels, n_leaf)),
         ],
         compiler_params=pltpu.CompilerParams(
-            collective_id=0, has_side_effects=True, vmem_limit_bytes=40 * 2**20
+            collective_id=0, has_side_effects=True, vmem_limit_bytes=62 * 2**20
         ),
     )(
-        local_dep.reshape(loc, fan),
-        top_dep.reshape(levels - 1, dep),
+        local_dep.reshape(loc, fan).T,
+        top_dep.reshape(levels - 1, dep).T,
         local_inv.reshape(loc, s, s),
         local_off.reshape(loc, fan * s, s),
         local_rhs.reshape(loc, r, s),

time: 83.9 us -> 74.8 us (0.89)
  local copies, waits for them, and re-layouts: 10.4 us -> 3.56 us
  Pallas kernels: 72.5 us -> 70.4 us
    unnamed x14 -> x2, local copies, waits for them, and re-layouts: 8.84 us -> 3.56 us
    pallas_call x1, Pallas kernels: 72.5 us -> 70.4 us  [on_device(): pl.pallas_call(functools.partial(kernel, sizes, chunk), out_shape=(jax.Sh...]
    reshape x2 -> x0, local copies, waits for them, and re-layouts: 1.52 us -> none  [the longest x1 0.77 us: on_device(): top_dep.reshape(levels - 1, dep)]
where the time goes in v2:
time: 74.8 us; the launch traced here: 74.6 us
  Pallas kernels  70.4 us (94%)
  local copies, waits for them, and re-layouts  3.56 us (5%)
    pallas_call x1, Pallas kernels, on_device(): pl.pallas_call(functools.partial(kernel, sizes, chunk), out_shape=(jax.Sh...  70.4 us
    unnamed x2, local copies, waits for them, and re-layouts  3.56 us

profile of v2, /device:TPU:0, one launch (start us, length us, event | category | flops | bytes accessed | tf_op | source)
XLA Modules:
  0.0 74.6 jit_solution(4439734868992237413)
XLA Ops:
  0.6 70.4 %shard_map.95 = (f32[16,64,128]{2,1,0:T(8,128)}, f32[8,64,128]{2,1,0:T(8,128)}) custom-call(s32[2,16]{1,0:T(2,128)} %bitcast.25, s32[4,7]{1,0:T(4,128)} %bitcast.24, f32[16,128,128]{2,1,0:T(8,128)} %bitcast.18, f32[16,256,128]{2,1,0:T(8,128)} %bitcast.16, f32[16,64,128]{2,1,0:T(8,128)} %bitcast.19, f32[8,128,128]{2,1,0:T(8,128)} %bitcast.20, ...), custom_call_target="tpu_custom_call" | custom-call | tf_op jit(solution)/shard_map/pallas_call | solution.py:306
  71.0 1.9 %copy.13 = f32[1,1,16,64,128]{4,3,2,1,0:T(8,128)} copy(f32[1,1,16,64,128]{4,3,2,1,0:T(8,128)} %bitcast.21) | data formatting | bytes 1048576
  72.9 1.7 %copy.14 = f32[8,1,1,64,128]{4,3,2,1,0:T(8,128)} copy(f32[8,1,1,64,128]{4,3,2,1,0:T(8,128)} %bitcast.23) | data formatting | bytes 524288
